TPU v7x, 32 devices: a whole 2x2x4 slice. The times are simulated.
32 devices in a mesh: clip: 8 (over z, y), frame: 4 (over x, core).
Axes of the slice: x: 2, y: 2, z: 4, core: 2. Of those that a mesh axis runs over, the one named last changes fastest.
Arguments:
- clips_in: bfloat16 [8, 8, 20, 20, 320], P('clip', 'frame'), may hold values from -6 to 6
- out_grad: bfloat16 [8, 8, 20, 20, 320], P('clip', 'frame'), may hold values from -6 to 6
- clip_side: int32 [8], P('clip'), may hold values from 14 to 20, as said below
- qkv_weight: float32 [960, 320], P('frame'), may hold values from -0.3125 to 0.3125
- proj_weight: float32 [320, 320], P('frame'), may hold values from -6 to 6
- up_weight: float32 [1280, 320], P('frame'), may hold values from -0.3125 to 0.3125
- down_weight: float32 [1280, 320], P('frame'), may hold values from -0.15625 to 0.15625
- qkv_moment: float32 [960, 320], P('frame'), may hold values from -512 to 512
- proj_moment: float32 [320, 320], P('frame'), may hold values from -512 to 512
- up_moment: float32 [1280, 320], P('frame'), may hold values from -512 to 512
- down_moment: float32 [1280, 320], P('frame'), may hold values from -512 to 512
- vectors: float32 [9, 320], replicated
- vector_mean: float32 [9, 320], replicated, may hold values from -48 to 48
- vector_square: float32 [9, 320], replicated, may hold values from 5.12 to 51.2
- up_bias: float32 [1280], replicated, may hold values from -3 to 3
- up_bias_mean: float32 [1280], replicated, may hold values from -48 to 48
- up_bias_square: float32 [1280], replicated, may hold values from 5.12 to 51.2
- conv_kernel: float32 [27, 320], replicated, may hold values from -1.25 to 1.25
- kernel_mean: float32 [27, 320], replicated, may hold values from -48 to 48
- kernel_square: float32 [27, 320], replicated, may hold values from 5.12 to 51.2
Outputs:
- block_out: bfloat16 [8, 8, 20, 20, 320], P('clip', 'frame')
- input_grad: float32 [8, 8, 20, 20, 320], P('clip', 'frame')
- qkv_moment_new: float32 [960, 320], P('frame')
- qkv_weight_new: float32 [960, 320], P('frame')
- proj_moment_new: float32 [320, 320], P('frame')
- proj_weight_new: float32 [320, 320], P('frame')
- up_moment_new: float32 [1280, 320], P('frame')
- up_weight_new: float32 [1280, 320], P('frame')
- down_moment_new: float32 [1280, 320], P('frame')
- down_weight_new: float32 [1280, 320], P('frame')
- vector_mean_new: float32 [9, 320], replicated
- vector_square_new: float32 [9, 320], replicated
- vectors_new: float32 [9, 320], replicated
- up_bias_mean_new: float32 [1280], replicated
- up_bias_square_new: float32 [1280], replicated
- up_bias_new: float32 [1280], replicated
- kernel_mean_new: float32 [27, 320], replicated
- kernel_square_new: float32 [27, 320], replicated
- kernel_new: float32 [27, 320], replicated
Inputs may be any that keep to these rules, and one draw needn't show every extreme that they name: `clip_side`: each entry is 14 or 20; both occur in every draw.
All inputs are finite; a program needn't handle non-finite values.
Results may differ from a plain program's by a relative error of at most 0.009.
The roundings to bfloat16 on the way count: a program that leaves them out, or rounds other values in their place, can miss the bound.
Values may be sent and summed in bfloat16 or wider, within the bound.
A program may use at most 128 MiB of HBM per device.

v0:
```python
import functools
import math

import jax
import jax.numpy as jnp
import numpy as np
from jax import lax
from jax.experimental import pallas as pl
from jax.experimental.pallas import tpu as pltpu
from jax.sharding import PartitionSpec as P

D = 320
HEADS = 5
HEAD_DIM = 64
PAIR = 2 * HEAD_DIM
WIDE = HEADS * PAIR
FF = 1280
NS_STEPS = 5
STEP = 10
CLIP_TOK = 3200
SHARE = 320

POLY_ONE = 3.4445
POLY_TWO = -4.775
POLY_THREE = 2.0315
LOG2E = math.log2(math.e)
SCORE_SCALE = HEAD_DIM**-0.5
MASKED = -1e30
MESH = pl.DeviceIdType.MESH
BF = jnp.bfloat16
F32 = jnp.float32
NT = (((1,), (1,)), ((), ()))
VMEM_SPEC = pl.BlockSpec(memory_space=pltpu.VMEM)


def dot_nt(left, right):
    return lax.dot_general(left, right, NT, preferred_element_type=F32)


def dot_nn(left, right):
    return jnp.dot(left, right, preferred_element_type=F32)


def lanes_of(rows):
    return lax.broadcasted_iota(jnp.int32, (rows, PAIR), 1)


CELL_AT = np.stack([np.arange(400) // 20, np.arange(400) % 20], axis=1).astype(np.float32)


def select_lanes(upper):
    row = lax.broadcasted_iota(jnp.int32, (D, WIDE), 0)
    col = lax.broadcasted_iota(jnp.int32, (D, WIDE), 1)
    source = lax.shift_left(lax.shift_right_logical(col, 7), 6) + (col & (HEAD_DIM - 1))
    half = col & HEAD_DIM
    return (source == row) & (half == (HEAD_DIM if upper else 0))


def flatten_frame(read_row, dst, base):
    for row in range(20):
        dst[base + 20 * row : base + 20 * row + 20, :] = read_row(row).astype(F32)


def build_slabs(center, edged, slot, flat, cells):
    blank = jnp.zeros((20, D), F32)
    edged[1, slot, 0:20, :] = blank
    edged[1, slot, 420:440, :] = blank
    edged[1, slot, 20:420, :] = flat
    center[1, slot] = flat
    col = cells[:, 1:2]
    for e, keep in ((0, col > 0.5), (2, col < 18.5)):
        moved = jnp.where(keep, edged[1, slot, 19 + e : 419 + e, :], 0.0)
        center[e, slot] = moved
        edged[e, slot, 0:20, :] = blank
        edged[e, slot, 420:440, :] = blank
        edged[e, slot, 20:420, :] = moved


def slab(center, edged, slot, b, e, start, size):
    if b == 1:
        return center[e, slot, pl.ds(start, size), :]
    return edged[e, slot, pl.ds(start + 20 * b, size), :]


def inside_of(side_ref, cells):
    side = side_ref[0].astype(F32) - 0.5
    return (cells[:, 0:1] < side) & (cells[:, 1:2] < side)


def norm_parts(rows):
    average = jnp.sum(rows, axis=-1, keepdims=True) * (1.0 / D)
    centered = rows - average
    variance = jnp.sum(centered * centered, axis=-1, keepdims=True) * (1.0 / D)
    scale = lax.rsqrt(variance + 1e-05)
    return centered * scale, scale


def frame_peers():
    f = lax.axis_index("frame")
    near = f + 1 - 2 * lax.rem(f, 2)
    across = lax.rem(f + 2, 4)
    return f, near, across, lax.rem(near + 2, 4)


def share_rows(rows, clips):
    return 16 * (-(-rows // (16 * clips)))


def greet_all(clips):
    barrier = pltpu.get_barrier_semaphore()
    for peer in frame_peers()[1:]:
        pl.semaphore_signal(barrier, inc=1, device_id={"frame": peer}, device_id_type=MESH)
    c = lax.axis_index("clip")

    def greet(step, carry):
        pl.semaphore_signal(
            barrier, inc=1, device_id={"clip": lax.rem(c + step, clips)}, device_id_type=MESH
        )
        return carry

    lax.fori_loop(1, clips, greet, 0)


def await_greetings(count):
    pl.semaphore_wait(pltpu.get_barrier_semaphore(), count)


def send(src, dst, send_sem, recv_sem, peer):
    return pltpu.make_async_remote_copy(
        src_ref=src,
        dst_ref=dst,
        send_sem=send_sem,
        recv_sem=recv_sem,
        device_id={"frame": peer},
        device_id_type=MESH,
    )


def halo_copies(first, last, halo, sems):
    f = lax.axis_index("frame")
    down = send(first, halo.at[1], sems.at[0, 0], sems.at[1, 0], jnp.maximum(f - 1, 0))
    up = send(last, halo.at[0], sems.at[0, 1], sems.at[1, 1], jnp.minimum(f + 1, 3))
    return down, up


def start_halos(down, up, halo):
    f = lax.axis_index("frame")

    @pl.when(f > 0)
    def _():
        down.start()

    @pl.when(f < 3)
    def _():
        up.start()

    @pl.when(f == 0)
    def _():
        halo[0] = jnp.zeros(halo.shape[1:], halo.dtype)

    @pl.when(f == 3)
    def _():
        halo[1] = jnp.zeros(halo.shape[1:], halo.dtype)


def wait_halos(down, up):
    f = lax.axis_index("frame")

    @pl.when(f > 0)
    def _():
        down.wait_send()
        up.wait_recv()

    @pl.when(f < 3)
    def _():
        up.wait_send()
        down.wait_recv()


EXP_SCALE = SCORE_SCALE * LOG2E


def tail_lanes(inside, copies):
    lane = lax.broadcasted_iota(jnp.int32, (inside.shape[0], PAIR), 1)
    tail = jnp.where(
        lane == HEAD_DIM,
        jnp.where(inside, 0.0, MASKED),
        jnp.where((lane > HEAD_DIM) & (lane < HEAD_DIM + 4), 1.0, 0.0),
    )
    return jnp.concatenate([tail] * copies, axis=0).astype(BF)


def front_kernel(
    clips,
    x_ref,
    side_ref,
    cells_ref,
    qkv_ref,
    proj_ref,
    up_ref,
    down_ref,
    vec_ref,
    taps_ref,
    tok_out,
    nhome_out,
    ncross_out,
    q_out,
    home_out,
    cross_out,
    kept_out,
    att_out,
    wq_out,
    wkv_out,
    others_out,
    tok_ref,
    nhome_ref,
    ncross_ref,
    q_ref,
    home_ref,
    cross_ref,
    kept_ref,
    att_ref,
    wq_ref,
    wkv_ref,
    others_ref,
    halo_ref,
    edge,
    raw,
    center,
    edged,
    qkv_full,
    tail,
    halo_sems,
    qkv_sems,
    other_sems,
    spread_sems,
    near_sems,
    cross_sems,
    out_sems,
):
    leaving = []

    def leave(src, dst):
        copy = pltpu.make_async_copy(src, dst, out_sems.at[len(leaving)])
        copy.start()
        leaving.append(copy)

    f, near, across, far = frame_peers()
    c = lax.axis_index("clip")
    greet_all(clips)
    part_rows = qkv_ref.shape[1]

    def qkv_rows(owner):
        return qkv_full.at[pl.ds(pl.multiple_of(owner * part_rows, 16), part_rows), :]

    qkv_full[pl.ds(pl.multiple_of(f * part_rows, 16), part_rows), :] = qkv_ref[...].T.astype(BF)
    start = 0
    for shard in (proj_ref, up_ref, down_ref):
        size = shard.shape[0]
        others_ref[f, start : start + size, :] = shard[...].astype(BF)
        start += size
    spare = others_ref.shape[1] - start
    if spare:
        others_ref[f, start : start + spare, :] = jnp.zeros((spare, D), BF)
    cells = cells_ref[...]
    inside = inside_of(side_ref, cells)
    for t in range(2):
        flatten_frame(lambda row, t=t: x_ref[0, row, :, t, :], raw, 400 * t)
        edge[t] = raw[400 * t : 400 * t + 400, :].astype(BF)

    await_greetings(3 + clips - 1)
    down, up = halo_copies(edge.at[0], edge.at[1], halo_ref, halo_sems)
    start_halos(down, up, halo_ref)
    qkv_cross = send(qkv_rows(f), qkv_rows(f), qkv_sems.at[0, 1], qkv_sems.at[1, 1], across)
    qkv_near = send(qkv_rows(f), qkv_rows(f), qkv_sems.at[0, 0], qkv_sems.at[1, 0], near)
    qkv_relay = send(
        qkv_rows(across), qkv_rows(across), qkv_sems.at[0, 2], qkv_sems.at[1, 2], near
    )
    qkv_near.start()

    part = others_ref.shape[1] // clips

    def part_of(owner, clip):
        return others_ref.at[owner, pl.ds(pl.multiple_of(clip * part, 16), part), :]

    other_near = send(
        others_ref.at[f], others_ref.at[f], other_sems.at[0, 0], other_sems.at[1, 0], near
    )
    other_cross = send(
        part_of(f, c), part_of(f, c), other_sems.at[0, 1], other_sems.at[1, 1], across
    )
    other_relay = send(
        others_ref.at[across],
        others_ref.at[across],
        other_sems.at[0, 2],
        other_sems.at[1, 2],
        near,
    )

    def spread(clip, landing):
        return pltpu.make_async_remote_copy(
            src_ref=part_of(across, c),
            dst_ref=part_of(across, landing),
            send_sem=spread_sems.at[0, clip],
            recv_sem=spread_sems.at[1, landing],
            device_id={"clip": clip},
            device_id_type=MESH,
        )

    def other_clips(act):
        def body(step, carry):
            act(lax.rem(c + step, clips))
            return carry

        lax.fori_loop(1, clips, body, 0)

    other_near.start()

    for t in range(2):
        build_slabs(
            center, edged, t + 1, jnp.where(inside, raw[400 * t : 400 * t + 400, :], 0.0), cells
        )

    def conv_part(t, depths, start, total):
        for a in depths:
            for b in range(3):
                for e in range(3):
                    offset = 9 * a + 3 * b + e
                    total = total + taps_ref[offset : offset + 1, :] * slab(
                        center, edged, t + a, b, e, start, 40
                    )
        return total

    for t, depths in ((0, (1, 2)), (1, (0, 1))):

        def own_part(step, carry, t=t, depths=depths):
            start = pl.multiple_of(step * 40, 8)
            at = pl.ds(pl.multiple_of(start + 400 * t, 8), 40)
            tok_ref[at, :] = conv_part(t, depths, start, raw[at, :] + vec_ref[4:5, :])
            return carry

        lax.fori_loop(0, 10, own_part, 0)
        if t == 0:
            qkv_cross.start()
            other_cross.start()
    wait_halos(down, up)
    for side, slot in ((0, 0), (1, 3)):
        rim = halo_ref[side].astype(F32)
        build_slabs(center, edged, slot, jnp.where(inside, rim, 0.0), cells)
    rows = tok_ref.shape[0]
    piece = rows // HEADS

    def cross_copy(k):
        at = pl.ds(pl.multiple_of(k * piece, 16), piece)
        return send(
            nhome_ref.at[at, :],
            ncross_ref.at[at, :],
            cross_sems.at[0, 0, k],
            cross_sems.at[1, 0, k],
            across,
        )

    def relay_copy(k):
        return send(
            ncross_ref.at[pl.ds(pl.multiple_of(k * piece, 16), piece), :],
            ncross_ref.at[pl.ds(pl.multiple_of(rows + k * piece, 16), piece), :],
            cross_sems.at[0, 1, k],
            cross_sems.at[1, 1, k],
            near,
        )

    near_copy = send(
        nhome_ref.at[pl.ds(0, rows), :],
        nhome_ref.at[pl.ds(rows, rows), :],
        near_sems.at[0],
        near_sems.at[1],
        near,
    )
    for t, depths, ready in ((0, (0,), (0, 1)), (1, (2,), (2, 3, 4))):

        def rim_part(step, carry, t=t, depths=depths):
            start = pl.multiple_of(step * 40, 8)
            at = pl.ds(pl.multiple_of(start + 400 * t, 8), 40)
            rows = conv_part(t, depths, start, tok_ref[at, :])
            tok_ref[at, :] = rows
            raw[at, :] = norm_parts(rows)[0] * vec_ref[0:1, :] + vec_ref[1:2, :]
            return carry

        lax.fori_loop(0, 10, rim_part, 0)
        at = slice(400 * t, 400 * t + 400)
        nhome_ref[at, :] = raw[at, :].astype(BF)
        for k in ready:
            cross_copy(k).start()
    near_copy.start()
    qkv_cross.wait_recv()
    qkv_relay.start()
    other_cross.wait_recv()
    other_clips(lambda clip: spread(clip, c).start())

    blank = jnp.zeros((1, HEAD_DIM), F32)

    def head_bias(row, h):
        return vec_ref[row : row + 1, HEAD_DIM * h : HEAD_DIM * (h + 1)]

    qkv_near.wait_recv()
    qkv_relay.wait_recv()
    for h in range(HEADS):
        wq_ref[PAIR * h : PAIR * h + HEAD_DIM, :] = qkv_full[HEAD_DIM * h : HEAD_DIM * (h + 1), :]
        wq_ref[PAIR * h + HEAD_DIM : PAIR * (h + 1), :] = jnp.zeros((HEAD_DIM, D), BF)
        wkv_ref[PAIR * h : PAIR * h + HEAD_DIM, :] = qkv_full[
            D + HEAD_DIM * h : D + HEAD_DIM * (h + 1), :
        ]
        wkv_ref[PAIR * h + HEAD_DIM : PAIR * (h + 1), :] = qkv_full[
            2 * D + HEAD_DIM * h : 2 * D + HEAD_DIM * (h + 1), :
        ]
    leave(tok_ref, tok_out)
    leave(wq_ref, wq_out)
    leave(wkv_ref, wkv_out)
    wide_query = jnp.concatenate(
        [part for h in range(HEADS) for part in (head_bias(5, h), blank)], axis=1
    )
    wide_pair = jnp.concatenate(
        [part for h in range(HEADS) for part in (blank, head_bias(6, h))], axis=1
    )

    def project(normed, weight, bias, place):
        joined = (dot_nt(normed, weight[...]) + bias).astype(BF)
        for h in range(HEADS):
            place(h, joined[:, PAIR * h : PAIR * (h + 1)])

    def place_query(h, value):
        q_ref[h] = value

    def place_own(h, value):
        home_ref[h, 0:rows, :] = value

    def place_near(h, value):
        home_ref[h, rows : 2 * rows, :] = value

    def place_cross(h, value):
        cross_ref[h] = value

    project(nhome_ref[0:rows, :], wq_ref, wide_query, place_query)
    project(nhome_ref[0:rows, :], wkv_ref, wide_pair, place_own)
    leave(q_ref, q_out)
    tail[...] = tail_lanes(inside, 4)
    tile = rows // 2
    mask_lane = jnp.where(lanes_of(tile) == HEAD_DIM, 1.0, 0.0).astype(BF)

    def tile_pass(t, source, last):
        at = pl.ds(pl.multiple_of(t * tile, 16), tile)
        lane = lanes_of(tile)
        for h in range(HEADS):
            keys = jnp.concatenate([source[h], tail[...]], axis=1)
            score = dot_nt(jnp.concatenate([q_ref[h, at, :], mask_lane], axis=1), keys)
            peak = jnp.max(score, axis=-1, keepdims=True)
            if last:
                kept = kept_ref[h, at, :]
                old_peak = kept[:, 0:1]
                peak = jnp.maximum(peak, old_peak)
            terms = jnp.exp2((score - peak) * EXP_SCALE).astype(BF)
            mixed = dot_nn(terms, keys)
            total = mixed[:, PAIR + HEAD_DIM + 1 : PAIR + HEAD_DIM + 2]
            mixed = mixed[:, 0:PAIR]
            if last:
                fade = jnp.exp2((old_peak - peak) * EXP_SCALE)
                total = total + fade * kept[:, 32:33]
                mixed = (mixed + fade * kept) / total
                log_sum = peak + jnp.log2(total) * (1.0 / EXP_SCALE)
                kept_ref[h, at, :] = jnp.where(lane < HEAD_DIM, log_sum, mixed)
                att_ref[h, at, :] = jnp.where(lane < HEAD_DIM, 0.0, mixed).astype(BF)
            else:
                kept_ref[h, at, :] = jnp.where(
                    lane < 32, peak, jnp.where(lane < HEAD_DIM, total, mixed)
                )

    def pass_on(k):
        cross_copy(k).wait_recv()
        relay_copy(k).start()

    def first_pass(t, carry):
        tile_pass(t, home_ref, False)

        @pl.when(t == 0)
        def _():
            for k in (0, 1, 2):
                pass_on(k)

        return carry

    def second_pass(t, carry):
        tile_pass(t, cross_ref, True)

        @pl.when(t == 0)
        def _():
            other_relay.wait_recv()
            others_leave.start()

        return carry

    near_copy.wait_recv()
    other_near.wait()
    leave(nhome_ref, nhome_out)
    project(nhome_ref[rows : 2 * rows, :], wkv_ref, wide_pair, place_near)
    leave(home_ref, home_out)
    lax.fori_loop(0, 2, first_pass, 0)
    for k in (3, 4):
        pass_on(k)
    other_clips(lambda clip: spread(clip, clip).wait_recv())
    other_relay.start()
    others_leave = pltpu.make_async_copy(others_ref, others_out, out_sems.at[out_sems.shape[0] - 1])
    for k in range(HEADS):
        relay_copy(k).wait_recv()
    leave(ncross_ref, ncross_out)
    project(ncross_ref[...], wkv_ref, wide_pair, place_cross)
    leave(cross_ref, cross_out)
    lax.fori_loop(0, 2, second_pass, 0)
    leave(kept_ref, kept_out)
    leave(att_ref, att_out)
    other_relay.wait_send()
    other_clips(lambda clip: spread(clip, c).wait_send())
    for copy in (other_cross, near_copy, qkv_cross, qkv_near, qkv_relay):
        copy.wait_send()
    for k in range(HEADS):
        cross_copy(k).wait_send()
        relay_copy(k).wait_send()
    others_leave.wait()
    for copy in leaving:
        copy.wait()


def front(clips_in, clip_side, qkv, proj, up, down, vectors, taps, clips, collective_id):
    rows = 800
    other_rows = clips * share_rows(proj.shape[0] + up.shape[0] + down.shape[0], clips)
    outs = (
        ((rows, D), F32),
        ((2 * rows, D), BF),
        ((2 * rows, D), BF),
        ((HEADS, rows, PAIR), BF),
        ((HEADS, 2 * rows, PAIR), BF),
        ((HEADS, 2 * rows, PAIR), BF),
        ((HEADS, rows, PAIR), F32),
        ((HEADS, rows, PAIR), BF),
        ((WIDE, D), BF),
        ((WIDE, D), BF),
        ((4, other_rows, D), BF),
    )
    return pl.pallas_call(
        functools.partial(front_kernel, clips),
        in_specs=[VMEM_SPEC, pl.BlockSpec(memory_space=pltpu.SMEM)] + [VMEM_SPEC] * 7,
        out_specs=[pl.BlockSpec(memory_space=pl.ANY)] * len(outs),
        out_shape=[jax.ShapeDtypeStruct(*out) for out in outs],
        scratch_shapes=[pltpu.VMEM(*out) for out in outs]
        + [
            pltpu.VMEM((2, 400, D), BF),
            pltpu.VMEM((2, 400, D), BF),
            pltpu.VMEM((rows, D), F32),
            pltpu.VMEM((3, 4, 400, D), F32),
            pltpu.VMEM((3, 4, 440, D), F32),
            pltpu.VMEM((3 * D, D), BF),
            pltpu.VMEM((2 * rows, PAIR), BF),
            pltpu.SemaphoreType.DMA((2, 2)),
            pltpu.SemaphoreType.DMA((2, 3)),
            pltpu.SemaphoreType.DMA((2, 3)),
            pltpu.SemaphoreType.DMA((2, clips)),
            pltpu.SemaphoreType.DMA((2,)),
            pltpu.SemaphoreType.DMA((2, 2, HEADS)),
            pltpu.SemaphoreType.DMA((len(outs),)),
        ],
        compiler_params=pltpu.CompilerParams(
            collective_id=collective_id, has_side_effects=True, vmem_limit_bytes=60 * 2**20
        ),
        cost_estimate=pl.CostEstimate(
            flops=2**34, bytes_accessed=16 * 2**20, transcendentals=2**23
        ),
    )(clips_in, clip_side, jnp.asarray(CELL_AT), qkv, proj, up, down, vectors, taps)


INV_SQRT2 = math.sqrt(0.5)
INV_SQRT_2PI = 1.0 / math.sqrt(2.0 * math.pi)


def dot_tn(left, right):
    return lax.dot_general(left, right, (((0,), (0,)), ((), ())), preferred_element_type=F32)


def norm_back(upstream, unit, scale, gain):
    through = upstream * gain
    mean_one = jnp.sum(through, axis=-1, keepdims=True) * (1.0 / D)
    mean_two = jnp.sum(through * unit, axis=-1, keepdims=True) * (1.0 / D)
    return scale * (through - mean_one - unit * mean_two)


def column_sum(rows):
    return jnp.sum(rows, axis=0, keepdims=True)


def mid_phase(
    att_ref,
    tok_ref,
    og_ref,
    side_ref,
    cells_ref,
    vec_ref,
    ubias_ref,
    others_ref,
    out_ref,
    gsec_ref,
    dout_ref,
    grads_ref,
    vsum_ref,
    raw,
    first_out,
    wide,
    act,
    ghid,
    normed,
    top,
    branch_low,
    att_low,
    proj_ref,
    up_ref,
    down_ref,
):
    start = 0
    for full in (proj_ref, up_ref, down_ref):
        size = full.shape[0] // 4
        for owner in range(4):
            full[size * owner : size * (owner + 1), :] = others_ref[owner, start : start + size, :]
        start += size
    up_bias = jnp.concatenate([ubias_ref[r : r + 1, :] for r in range(FF // 128)], axis=1)
    inside = inside_of(side_ref, cells_ref[...])
    pick = select_lanes(True).astype(F32).astype(BF)
    wide[...] = dot_nn(proj_ref[...], pick).astype(BF)
    vsum_ref[...] = jnp.zeros(vsum_ref.shape, F32)
    for t in range(2):
        at = slice(400 * t, 400 * t + 400)
        heads = jnp.concatenate([att_ref[h, at, :] for h in range(HEADS)], axis=1)
        att_low[at, :] = dot_nt(heads, pick).astype(BF)
        second = tok_ref[at, :] + (dot_nt(heads, wide[...]) + vec_ref[7:8, :])
        unit, scale = norm_parts(second)
        normed_two = (unit * vec_ref[2:3, :] + vec_ref[3:4, :]).astype(BF)
        normed[at, :] = normed_two
        flatten_frame(lambda row, t=t: og_ref[0, row, :, t, :], raw, 0)
        grad_top = jnp.where(inside, raw[...], 0.0)
        top_low = grad_top.astype(BF)
        top[at, :] = top_low
        hidden = dot_nt(normed_two, up_ref[...]) + up_bias
        half = 0.5 + 0.5 * lax.erf(hidden * INV_SQRT2)
        activated = (hidden * half).astype(BF)
        act[at, :] = activated
        slope = half + hidden * (INV_SQRT_2PI * jnp.exp(-0.5 * hidden * hidden))
        grad_hidden = (dot_nt(top_low, down_ref[...]) * slope).astype(BF)
        ghid[at, :] = grad_hidden
        result = second + (dot_nn(activated, down_ref[...]) + vec_ref[8:9, :])
        if t == 0:
            first_out[...] = result
        else:
            raw[...] = result
            for row in range(20):
                part = slice(20 * row, 20 * row + 20)
                out_ref[0, row] = jnp.stack([first_out[part, :], raw[part, :]], axis=1).astype(BF)
        upstream = dot_nn(grad_hidden, up_ref[...])
        grad_second = grad_top + norm_back(upstream, unit, scale, vec_ref[2:3, :])
        gsec_ref[at, :] = grad_second
        low = grad_second.astype(BF)
        branch_low[at, :] = low
        dout = dot_nn(low, wide[...]).astype(BF)
        for h in range(HEADS):
            dout_ref[h, at, :] = dout[:, PAIR * h : PAIR * (h + 1)]
        vsum_ref[0:1, :] += column_sum(upstream * unit)
        vsum_ref[1:2, :] += column_sum(upstream)
        vsum_ref[2:3, :] += column_sum(low.astype(F32))
        vsum_ref[3:4, :] += column_sum(grad_top)
        bias_sum = column_sum(grad_hidden.astype(F32))
        for part in range(4):
            vsum_ref[4 + part : 5 + part, :] += bias_sum[:, D * part : D * (part + 1)]
    rows = up_ref.shape[0] // 4
    proj_rows = D // 4
    grad = dot_tn(branch_low[...], att_low[...]).astype(BF)
    for owner in range(4):
        grads_ref[owner, 0:proj_rows, :] = grad[proj_rows * owner : proj_rows * (owner + 1), :]
    for owner in range(4):
        at = slice(rows * owner, rows * (owner + 1))
        start = proj_rows
        grads_ref[owner, start : start + rows, :] = dot_tn(ghid[:, at], normed[...]).astype(BF)
        start = proj_rows + rows
        grads_ref[owner, start : start + rows, :] = dot_tn(act[:, at], top[...]).astype(BF)


class RowSums:
    def __init__(self, clips, g_ref, at, pair_in, cross_out, cross_in, shares, shares_in, sums,
                 frame_sems, part_sems, sum_sems):
        self.clips = clips
        self.g = g_ref
        self.at = at
        self.pair_in = pair_in
        self.cross_out = cross_out
        self.cross_in = cross_in
        self.shares = shares
        self.shares_in = shares_in
        self.sums = sums
        self.part_sems = part_sems
        self.sum_sems = sum_sems
        f, near, across, far = frame_peers()
        self.f, self.across = f, across
        self.c = lax.axis_index("clip")
        sem = frame_sems
        part = lambda owner: g_ref.at[owner, pl.ds(at.start, at.stop - at.start), :]
        self.first = send(part(far), pair_in.at[0], sem.at[0, 0], sem.at[1, 0], near)
        self.second = send(part(near), pair_in.at[1], sem.at[0, 1], sem.at[1, 1], near)
        self.cross = send(cross_out, cross_in, sem.at[0, 2], sem.at[1, 2], across)

    def peer(self, step):
        return lax.rem(self.c + step, self.clips)

    def part_copy(self, step):
        return pltpu.make_async_remote_copy(
            src_ref=self.shares.at[self.peer(step)],
            dst_ref=self.shares_in.at[step],
            send_sem=self.part_sems.at[0, step],
            recv_sem=self.part_sems.at[1, step],
            device_id={"clip": self.peer(step)},
            device_id_type=MESH,
        )

    def sum_copy(self, step):
        return pltpu.make_async_remote_copy(
            src_ref=self.sums.at[self.c],
            dst_ref=self.sums.at[self.c],
            send_sem=self.sum_sems.at[0, step],
            recv_sem=self.sum_sems.at[1, step],
            device_id={"clip": self.peer(step)},
            device_id_type=MESH,
        )

    def each(self, act):
        def body(step, carry):
            act(step)
            return carry

        lax.fori_loop(1, self.clips, body, 0)

    def pair_step(self):
        self.first.start()
        self.second.start()

    def cross_step(self):
        self.first.wait()
        self.cross_out[...] = (
            self.g[self.across, self.at, :].astype(F32) + self.pair_in[0].astype(F32)
        ).astype(BF)
        self.cross.start()

    def share_step(self):
        self.second.wait()
        self.cross.wait()
        mine = (
            self.g[self.f, self.at, :].astype(F32)
            + self.pair_in[1].astype(F32)
            + self.cross_in[...].astype(F32)
        ).astype(BF)
        rows, chunk = mine.shape[0], self.shares.shape[1]
        spare = self.clips * chunk - rows
        if spare:
            mine = jnp.concatenate([mine, jnp.zeros((spare, D), BF)], axis=0)
        self.shares[...] = mine.reshape(self.clips, chunk, D)
        self.each(lambda step: self.part_copy(step).start())

    def sum_step(self):
        self.each(lambda step: self.part_copy(step).wait())

        def add_part(step, total):
            return total + self.shares_in[step].astype(F32)

        total = lax.fori_loop(1, self.clips, add_part, self.shares[self.c].astype(F32))
        self.sums[self.c] = total.astype(BF)
        self.each(lambda step: self.sum_copy(step).start())

    def finish(self):
        self.each(lambda step: self.sum_copy(step).wait())


def row_sums_scratch(rows, clips):
    chunk = share_rows(rows, clips)
    return [
        pltpu.VMEM((2, rows, D), BF),
        pltpu.VMEM((rows, D), BF),
        pltpu.VMEM((rows, D), BF),
        pltpu.VMEM((clips, chunk, D), BF),
        pltpu.VMEM((clips, chunk, D), BF),
        pltpu.VMEM((clips, chunk, D), BF),
        pltpu.SemaphoreType.DMA((2, 3)),
        pltpu.SemaphoreType.DMA((2, clips)),
        pltpu.SemaphoreType.DMA((2, clips)),
    ]


EARLY_PARTS = (slice(0, 400), slice(400, 720))


def row_pieces(start, size, block):
    pieces, skip = [], 0
    while skip < size:
        owner, row = divmod(start + skip, block)
        step = min(size - skip, block - row)
        pieces.append((owner, row, skip, step))
        skip += step
    return pieces


def back_phase(
    one,
    two,
    arrived,
    q_ref,
    dout_ref,
    kept_ref,
    cross_ref,
    home_ref,
    nhome_ref,
    ncross_ref,
    wq_ref,
    wkv_ref,
    side_ref,
    cells_ref,
    gnorm_ref,
    own_ref,
    out_ref,
    bsum_ref,
    grads_ref,
    grads_in,
    pair_out,
    pair_in,
    cross_out,
    cross_in,
    pair_sems,
    cross_sems,
    grad_sems,
    extra,
    qd_t,
    tail,
    low_one,
    low_two,
    low_three,
    dq_sum,
    turned_pairs,
    pair_grad,
):
    f, near, across, far = frame_peers()
    rows = q_ref.shape[1]
    dnormed = gnorm_ref
    dq_low = q_ref
    tail[...] = tail_lanes(inside_of(side_ref, cells_ref[...]), 4)
    arrived(0, 3)
    lower = lax.broadcasted_iota(jnp.int32, (PAIR, 1), 0) < HEAD_DIM
    scale_of = jnp.where(lower, SCORE_SCALE, 1.0)
    chunks = ((0, 512, low_one), (512, 512, low_two), (1024, 576, low_three))

    def minus_parts(column, lane):
        high = column.astype(BF).astype(F32)
        mid = (column - high).astype(BF).astype(F32)
        rest = column - high - mid
        return jnp.where(
            lane == HEAD_DIM + 1,
            -high,
            jnp.where(lane == HEAD_DIM + 2, -mid, jnp.where(lane == HEAD_DIM + 3, -rest, 0.0)),
        )

    def prepare(h):
        lane = lanes_of(rows)
        kept = kept_ref[h]
        queries, douts = q_ref[h].astype(F32), dout_ref[h].astype(F32)
        log_sum = kept[:, 0:1]
        row_dot = jnp.sum(douts * kept, axis=-1, keepdims=True)
        of_queries = jnp.where(lane == HEAD_DIM, 1.0, minus_parts(log_sum, lane))
        extra[h, 0:rows, :] = of_queries.astype(BF)
        extra[h, rows : 2 * rows, :] = minus_parts(row_dot, lane).astype(BF)
        qd_t[h] = jnp.concatenate([queries, douts], axis=0).T.astype(BF)
        bsum_ref[1, h] = column_sum(douts)

    def head_pass(h, source, add):
        pairs = source[h]
        both = jnp.concatenate([q_ref[h], dout_ref[h]], axis=0)
        both = jnp.concatenate([both, extra[h]], axis=1)
        products = [
            dot_nt(
                both,
                jnp.concatenate(
                    [pairs[start : start + size, :], tail[start : start + size, :]], axis=1
                ),
            )
            for start, size, low in chunks
        ]
        total = dq_sum[h] if add else None
        at = pl.ds(pl.multiple_of(h * PAIR, PAIR), PAIR)
        for (start, size, low), product in zip(chunks, products):
            probs = jnp.exp2(product[0:rows, :] * EXP_SCALE)
            low[0:rows, :] = (probs * product[rows : 2 * rows, :]).astype(BF)
            low[rows : 2 * rows, :] = probs.astype(BF)
            part = dot_nn(low[0:rows, :], pairs[start : start + size, :])
            total = part if total is None else total + part
            turned = dot_nn(qd_t[h], low[...]) * scale_of
            turned_pairs[at, start : start + size] = turned.astype(BF)
        if add:
            total = jnp.where(lanes_of(rows) < HEAD_DIM, total * SCORE_SCALE, 0.0)
            dq_low[h] = total.astype(BF)
            bsum_ref[0, h] = column_sum(total)
        else:
            dq_sum[h] = total

    def of_normed(normed, add):
        grad = dot_nn(turned_pairs[...], normed[...])
        pair_grad[...] = pair_grad[...] + grad if add else grad
        total = dot_nn(wkv_ref[...].astype(F32).T.astype(BF), turned_pairs[...]).T
        dnormed[...] = total[0:rows, :]
        pair_out[...] = total[rows : 2 * rows, :].astype(BF)

    def pair_copy(phase):
        return send(
            pair_out, pair_in.at[phase], pair_sems.at[0, phase], pair_sems.at[1, phase], near
        )

    to_across = send(cross_out, cross_in, cross_sems.at[0], cross_sems.at[1], across)

    def cross_pass(h, carry):
        prepare(h)
        head_pass(h, cross_ref, False)

        @pl.when(h == 0)
        def _():
            one.cross_step()
            two.cross_step()

        @pl.when(h == 3)
        def _():
            one.share_step()

        return carry

    def home_pass(h, carry):
        head_pass(h, home_ref, True)

        @pl.when(h == 0)
        def _():
            pair_copy(0).wait()
            cross_out[...] = (dnormed[...] + pair_in[0].astype(F32)).astype(BF)
            to_across.start()
            two.share_step()

        @pl.when(h == 1)
        def _():
            one.sum_step()

        @pl.when(h == 3)
        def _():
            two.sum_step()

        return carry

    lax.fori_loop(0, HEADS, cross_pass, 0)
    arrived(3, 8)
    of_normed(ncross_ref, False)
    pair_copy(0).start()
    lax.fori_loop(0, HEADS, home_pass, 0)
    of_normed(nhome_ref, True)
    pair_copy(1).start()

    block = grads_ref.shape[1]

    def place(start, values):
        for owner, row, skip, size in row_pieces(start, values.shape[0], block):
            grads_ref[owner, row : row + size, :] = values[skip : skip + size, :]

    dq = jnp.concatenate([dq_low[h] for h in range(HEADS)], axis=1)
    of_queries = dot_tn(dq, nhome_ref[0:rows, :]).astype(BF)
    for h in range(HEADS):
        of_pairs = pair_grad[PAIR * h : PAIR * (h + 1), :].astype(BF)
        place(HEAD_DIM * h, of_queries[PAIR * h : PAIR * h + HEAD_DIM, :])
        place(D + HEAD_DIM * h, of_pairs[0:HEAD_DIM, :])
        place(2 * D + HEAD_DIM * h, of_pairs[HEAD_DIM:PAIR, :])
    to_pair = [
        send(grads_ref.at[peer], grads_in.at[k], grad_sems.at[0, k], grad_sems.at[1, k], near)
        for k, peer in enumerate((far, near))
    ]
    for copy in to_pair:
        copy.start()
    total = dnormed[...] + dot_nn(dq, wq_ref[...])
    to_across.wait()
    pair_copy(1).wait()
    gnorm_ref[...] = total + pair_in[1].astype(F32) + cross_in[...].astype(F32)
    for copy in to_pair:
        copy.wait()
    out_ref[...] = (grads_ref[across].astype(F32) + grads_in[0].astype(F32)).astype(BF)
    own_ref[...] = grads_ref[f].astype(F32) + grads_in[1].astype(F32)


def newton_schulz(whole):
    wide = whole.astype(F32)
    norm = jnp.sqrt(jnp.sum(wide * wide)) + 1e-07
    eye = (
        lax.broadcasted_iota(jnp.int32, (D, D), 0) == lax.broadcasted_iota(jnp.int32, (D, D), 1)
    ).astype(F32)
    turned = dot_nt(eye.astype(BF), whole) / norm

    def iterate(step, current):
        held = current.astype(BF)
        gram = dot_nt(held, held)
        gram_low = gram.astype(BF)
        poly = POLY_TWO * gram + POLY_THREE * dot_nn(gram_low, gram_low)
        return POLY_ONE * current + dot_nn(poly.astype(BF), held)

    return lax.fori_loop(0, NS_STEPS, iterate, turned)


OWNER_OF = (3, 1, 0, 2)
QKV_AT = OWNER_OF[0]


def tail_phase(
    clips,
    one,
    two,
    arrived,
    copy_out,
    gnorm_ref,
    own_ref,
    across_ref,
    bsum_ref,
    tok_ref,
    gsec_ref,
    x_ref,
    side_ref,
    cells_ref,
    taps_ref,
    vec_ref,
    mid_sums_ref,
    one_ref,
    two_ref,
    qkv_m_ref,
    proj_m_ref,
    up_m_ref,
    down_m_ref,
    late_ref,
    scaled_ref,
    vsum_ref,
    cross_in,
    shares,
    shares_in,
    new_rows,
    new_low,
    first_low,
    rim,
    v_mine,
    v_frames,
    v_total,
    v_clips,
    gathered,
    old_rows,
    center,
    edged,
    low,
    grad_sems,
    part_sems,
    row_sems,
    spread_sems,
    rim_sems,
    vf_sems,
    vc_sems,
    there_sems,
    back_sems,
):
    first, ingrad_ref, outer = gnorm_ref, gsec_ref, tok_ref
    f, near, across, far = frame_peers()
    c = lax.axis_index("clip")
    block = own_ref.shape[0]
    owners, chunk = shares.shape[0], shares.shape[1]

    def each(count, act):
        def body(step, carry):
            act(step)
            return carry

        lax.fori_loop(0, count, body, 0)

    def other_clips(act):
        each(clips - 1, lambda step: act(lax.rem(c + 1 + step, clips)))

    down, up = halo_copies(first_low.at[0], first_low.at[1], rim, rim_sems)

    to_across = send(across_ref, cross_in, grad_sems.at[0], grad_sems.at[1], across)
    to_across.start()

    upstream = gnorm_ref[...]
    unit, scale = norm_parts(tok_ref[...])
    grad_first = gsec_ref[...] + norm_back(upstream, unit, scale, vec_ref[0:1, :])
    first[...] = grad_first
    first_low[...] = grad_first.astype(BF).reshape(first_low.shape)
    one.finish()
    two.finish()
    one_ref[...] = one.sums[...].reshape(one_ref.shape)
    two_ref[...] = two.sums[...].reshape(two_ref.shape)
    arrived(0, 5)
    old_rows[0:block, :] = qkv_m_ref[...].T
    if owners * chunk > block:
        old_rows[block : owners * chunk, :] = jnp.zeros((owners * chunk - block, D), F32)

    v_mine[0:1, :] = column_sum(upstream * unit)
    v_mine[1:2, :] = column_sum(upstream)
    v_mine[2:4, :] = mid_sums_ref[0:2, :]
    v_mine[4:5, :] = column_sum(grad_first)
    v_mine[5:6, :] = jnp.concatenate(
        [bsum_ref[0, h, :, 0:HEAD_DIM] for h in range(HEADS)], axis=1
    )
    v_mine[6:7, :] = jnp.concatenate(
        [bsum_ref[1, h, :, HEAD_DIM:PAIR] for h in range(HEADS)], axis=1
    )
    v_mine[7:9, :] = mid_sums_ref[2:4, :]
    v_mine[9:13, :] = mid_sums_ref[4:8, :]

    cells = cells_ref[...]
    inside = inside_of(side_ref, cells)
    for t in range(2):
        build_slabs(center, edged, t + 1, first[400 * t : 400 * t + 400, :], cells)

    def part_copy(owner):
        return pltpu.make_async_remote_copy(
            src_ref=shares.at[owner],
            dst_ref=shares_in.at[c],
            send_sem=part_sems.at[0, owner],
            recv_sem=part_sems.at[1, c],
            device_id={"clip": owner},
            device_id_type=MESH,
        )

    def other_owners(act):
        def step(owner):
            @pl.when(owner != c)
            def _():
                act(owner)

        each(owners, step)

    to_across.wait()
    mine = (own_ref[...] + cross_in[...].astype(F32)).astype(BF)
    if owners * chunk > block:
        mine = jnp.concatenate([mine, jnp.zeros((owners * chunk - block, D), BF)], axis=0)
    shares[...] = mine.reshape(owners, chunk, D)
    other_owners(lambda owner: part_copy(owner).start())
    start_halos(down, up, rim)

    moments = (None, proj_m_ref, up_m_ref, down_m_ref)

    def to_owner(which):
        at = pl.ds(0, moments[which].shape[0])
        return send(
            low.at[which, at, :],
            gathered.at[f, at, :],
            there_sems.at[0, which],
            there_sems.at[1, f],
            OWNER_OF[which],
        )

    for which in (3, 2, 1):
        rows = moments[which].shape[0]
        summed = one_ref[80:400, :] if which == 2 else (two_ref if which == 3 else one_ref)[0:rows, :]
        low[which, 0:rows, :] = (0.95 * moments[which][...] + summed.astype(F32)).astype(BF)

        @pl.when(f != OWNER_OF[which])
        def _(which=which):
            to_owner(which).start()

    def row_copy(clip):
        return pltpu.make_async_remote_copy(
            src_ref=new_rows.at[c],
            dst_ref=new_rows.at[c],
            send_sem=row_sems.at[0, clip],
            recv_sem=row_sems.at[1, c],
            device_id={"clip": clip},
            device_id_type=MESH,
        )

    def spread_copy(clip):
        return pltpu.make_async_remote_copy(
            src_ref=new_low,
            dst_ref=gathered.at[f, pl.ds(pl.multiple_of(c * chunk, 16), chunk), :],
            send_sem=spread_sems.at[4, clip],
            recv_sem=spread_sems.at[f, c],
            device_id={"clip": clip, "frame": QKV_AT},
            device_id_type=MESH,
        )

    def share_sum():
        @pl.when(c < owners)
        def _():
            shares_in[c] = shares[c]

            def arrive(clip):
                pltpu.make_async_remote_copy(
                    src_ref=shares.at[0],
                    dst_ref=shares_in.at[clip],
                    send_sem=part_sems.at[0, 0],
                    recv_sem=part_sems.at[1, clip],
                    device_id={"clip": clip},
                    device_id_type=MESH,
                ).wait_recv()

            other_clips(arrive)

            def add_part(clip, total):
                return total + shares_in[clip].astype(F32)

            total = lax.fori_loop(0, clips, add_part, jnp.zeros((chunk, D), F32))
            at = pl.ds(pl.multiple_of(c * chunk, 16), chunk)
            fresh = 0.95 * old_rows[at, :] + total
            new_rows[c] = fresh
            new_low[...] = fresh.astype(BF)
            other_clips(lambda clip: spread_copy(clip).start())

            @pl.when(f != QKV_AT)
            def _():
                spread_copy(c).start()

            @pl.when(f == QKV_AT)
            def _():
                gathered[QKV_AT, at, :] = new_low[...]

            other_clips(lambda clip: row_copy(clip).start())

    for t in range(2):
        at = slice(400 * t, 400 * t + 400)
        flatten_frame(lambda row, t=t: x_ref[0, row, :, t, :], outer, 400 * t)
        outer[at, :] = jnp.where(inside, outer[at, :], 0.0)

    def plane(t, a, add_rows, add_taps):
        def step(number, totals):
            start = pl.multiple_of(number * 16, 16)
            at = pl.ds(pl.multiple_of(start + 400 * t, 16), 16)
            masked = outer[at, :]
            total = jnp.zeros((16, D), F32)
            sums_out = []
            for b in range(3):
                for e in range(3):
                    offset = 9 * a + 3 * b + e
                    piece = slab(center, edged, t + 2 - a, 2 - b, 2 - e, start, 16)
                    total = total + taps_ref[offset : offset + 1, :] * piece
                    product = masked * piece
                    sums_out.append(totals[3 * b + e] + (product[0:8, :] + product[8:16, :]))
            if add_rows:
                ingrad_ref[at, :] += total
            else:
                ingrad_ref[at, :] = total
            return tuple(sums_out)

        totals = lax.fori_loop(0, 25, step, tuple(jnp.zeros((8, D), F32) for _ in range(9)))
        for which, total in enumerate(totals):
            at = slice(13 + 9 * a + which, 14 + 9 * a + which)
            if add_taps:
                v_mine[at, :] += column_sum(total)
            else:
                v_mine[at, :] = column_sum(total)

    plane(0, 0, False, False)
    plane(0, 1, True, False)
    share_sum()
    plane(1, 1, False, True)
    plane(1, 2, True, False)
    wait_halos(down, up)
    for side, slot in ((0, 0), (1, 3)):
        build_slabs(center, edged, slot, rim[side].astype(F32), cells)
    plane(0, 2, True, True)
    plane(1, 0, True, True)
    for t in range(2):
        at = slice(400 * t, 400 * t + 400)
        ingrad_ref[at, :] = first[at, :] + jnp.where(inside, ingrad_ref[at, :], 0.0)
    copy_out()

    v_copies = []
    for which, peer in enumerate((near, across, far)):
        copy = send(v_mine, v_frames.at[f], vf_sems.at[0, which], vf_sems.at[1, which], peer)
        copy.start()
        v_copies.append(copy)
    v_frames[f] = v_mine[...]

    @pl.when(f == QKV_AT)
    def _():
        def rows_arrive(frame, clip):
            pltpu.make_async_remote_copy(
                src_ref=new_low,
                dst_ref=gathered.at[frame, pl.ds(pl.multiple_of(clip * chunk, 16), chunk), :],
                send_sem=spread_sems.at[4, clip],
                recv_sem=spread_sems.at[frame, clip],
                device_id={"clip": clip, "frame": frame},
                device_id_type=MESH,
            ).wait_recv()

        other_owners(lambda clip: rows_arrive(QKV_AT, clip))
        for step in (1, 2, 3):
            frame = (QKV_AT + step) % 4
            each(owners, lambda clip, frame=frame: rows_arrive(frame, clip))

    for which in (1, 2, 3):

        @pl.when(f != OWNER_OF[which])
        def _(which=which):
            to_owner(which).wait_send()

        @pl.when(f == OWNER_OF[which])
        def _(which=which):
            at = pl.ds(0, moments[which].shape[0])
            gathered[OWNER_OF[which], at, :] = low[which, at, :]
            for other in range(4):
                if other != OWNER_OF[which]:
                    send(
                        low.at[0, at, :],
                        gathered.at[other, at, :],
                        there_sems.at[0, 0],
                        there_sems.at[1, other],
                        other,
                    ).wait_recv()

    turned = newton_schulz(gathered[...].reshape(4 * SHARE, D))
    low[:, 0:SHARE, :] = turned.T.astype(BF).reshape(4, SHARE, D)
    row_counts = (block, *(ref.shape[0] for ref in moments[1:]))

    def back_copy(which, step):
        at = pl.ds(0, row_counts[which])
        to = (OWNER_OF[which] + step) % 4
        return send(
            low.at[to, at, :],
            scaled_ref.at[which, at, :],
            back_sems.at[0, step],
            back_sems.at[1, which],
            to,
        )

    for which in range(4):

        @pl.when(f == OWNER_OF[which])
        def _(which=which):
            for step in (2, 1, 3):
                back_copy(which, step).start()
            at = pl.ds(0, row_counts[which])
            scaled_ref[which, at, :] = low[OWNER_OF[which], at, :]

    for copy in v_copies:
        copy.wait()
    v_total[...] = v_frames[0] + v_frames[1] + v_frames[2] + v_frames[3]

    def v_copy(clip):
        return pltpu.make_async_remote_copy(
            src_ref=v_total,
            dst_ref=v_clips.at[c],
            send_sem=vc_sems.at[0, clip],
            recv_sem=vc_sems.at[1, c],
            device_id={"clip": clip},
            device_id_type=MESH,
        )

    other_clips(lambda clip: v_copy(clip).start())
    v_clips[c] = v_total[...]

    other_owners(lambda owner: part_copy(owner).wait_send())

    @pl.when(c < owners)
    def _():
        other_clips(lambda clip: spread_copy(clip).wait_send())

        @pl.when(f != QKV_AT)
        def _():
            spread_copy(c).wait_send()

        other_clips(lambda clip: row_copy(clip).wait_send())

    def new_rows_arrive(clip):
        pltpu.make_async_remote_copy(
            src_ref=new_rows.at[0],
            dst_ref=new_rows.at[clip],
            send_sem=row_sems.at[0, 0],
            recv_sem=row_sems.at[1, clip],
            device_id={"clip": clip},
            device_id_type=MESH,
        ).wait_recv()

    other_owners(new_rows_arrive)
    late_ref[...] = new_rows[...].reshape(late_ref.shape)

    def v_arrives(clip):
        v_copy(clip).wait_send()
        pltpu.make_async_remote_copy(
            src_ref=v_total,
            dst_ref=v_clips.at[clip],
            send_sem=vc_sems.at[0, clip],
            recv_sem=vc_sems.at[1, clip],
            device_id={"clip": clip},
            device_id_type=MESH,
        ).wait_recv()

    other_clips(v_arrives)

    def add_v(step, total):
        return total + v_clips[step]

    vsum_ref[...] = lax.fori_loop(0, clips, add_v, jnp.zeros(vsum_ref.shape, F32))
    for which in range(4):

        @pl.when(f == OWNER_OF[which])
        def _(which=which):
            for step in (2, 1, 3):
                back_copy(which, step).wait_send()

        @pl.when(f != OWNER_OF[which])
        def _(which=which):
            back_copy(which, 1).wait_recv()


def rest_kernel(
    clips,
    att_in,
    tok_in,
    og_in,
    others_in,
    side_ref,
    cells_ref,
    vec_ref,
    ubias_ref,
    taps_ref,
    *refs,
):
    refs = list(refs)

    def take(count):
        taken, refs[:count] = refs[:count], []
        return taken

    back_sources = take(8)
    tail_sources = take(5)
    block_out, ingrad_out, one_ref, two_ref, late_ref, scaled_ref, vsum_ref = take(7)
    tok, out, gsec, dout, early, mid_sums = take(6)
    back_inputs = take(8)
    gnorm, own, across_rows, bsum = take(4)
    back_buffers = take(6)
    back_sems = take(3)
    tail_landing = take(12)
    tail_sems = take(9)
    (copy_sems,) = take(1)
    half = len(refs) // 2
    f, near, across, far = frame_peers()
    c = lax.axis_index("clip")
    gathered = tail_landing[-1]
    block, proj_rows = own.shape[0], D // 4
    chunk = share_rows(block, clips)
    owned = -(-block // chunk) * chunk

    @pl.when(f == QKV_AT)
    def _():
        gathered[:, owned:SHARE, :] = jnp.zeros((4, SHARE - owned, D), BF)

    @pl.when(f == OWNER_OF[1])
    def _():
        gathered[:, proj_rows:SHARE, :] = jnp.zeros((4, SHARE - proj_rows, D), BF)

    greet_all(clips)
    barrier = pltpu.get_barrier_semaphore()

    def greet(frame):
        def body(step, carry):
            pl.semaphore_signal(
                barrier,
                inc=1,
                device_id={"clip": lax.rem(c + step, clips), "frame": frame},
                device_id_type=MESH,
            )
            return carry

        lax.fori_loop(1, clips, body, 0)

    @pl.when(f == QKV_AT)
    def _():
        for step in (1, 2, 3):
            greet((QKV_AT + step) % 4)

    @pl.when(f != QKV_AT)
    def _():
        greet(QKV_AT)

    def copies(sources, targets, first):
        return [
            pltpu.make_async_copy(src, dst, copy_sems.at[first + k])
            for k, (src, dst) in enumerate(zip(sources, targets))
        ]

    def arrival(waiting):
        def arrived(start, stop):
            for copy in waiting[start:stop]:
                copy.wait()

        return arrived

    for_back = copies(back_sources, back_inputs, 4)

    def middle(att, og, others, *scratch):
        for_mid = copies((others_in, att_in, tok_in, og_in), (others, att, tok, og), 0)
        for copy in for_mid:
            copy.start()
        for copy in for_mid:
            copy.wait()
        for copy in for_back:
            copy.start()
        mid_phase(
            att, tok, og, side_ref, cells_ref, vec_ref, ubias_ref, others, out, gsec, dout, early,
            mid_sums, *scratch,
        )

    rows = tok.shape[0]
    vmem = pltpu.VMEM
    pl.run_scoped(
        middle,
        vmem(att_in.shape, BF),
        vmem(og_in.shape, BF),
        vmem(others_in.shape, BF),
        vmem((400, D), F32),
        vmem((400, D), F32),
        vmem((D, WIDE), BF),
        vmem((rows, FF), BF),
        vmem((rows, FF), BF),
        vmem((rows, D), BF),
        vmem((rows, D), BF),
        vmem((rows, D), BF),
        vmem((rows, D), BF),
        vmem((D, D), BF),
        vmem((FF, D), BF),
        vmem((FF, D), BF),
    )
    out_copy = pltpu.make_async_copy(out, block_out, copy_sems.at[0])
    out_copy.start()

    @pl.when(f == QKV_AT)
    def _():
        await_greetings(3 + 4 * (clips - 1))

    @pl.when(f != QKV_AT)
    def _():
        await_greetings(3 + 2 * (clips - 1))

    one = RowSums(clips, early, EARLY_PARTS[0], *refs[:half])
    two = RowSums(clips, early, EARLY_PARTS[1], *refs[half:])
    one.pair_step()
    two.pair_step()

    def backward(*scratch):
        back_phase(
            one, two, arrival(for_back), back_inputs[0], dout, *back_inputs[1:], side_ref,
            cells_ref, gnorm, own, across_rows, bsum, *back_buffers, *back_sems, *scratch,
        )

    pl.run_scoped(
        backward,
        vmem((HEADS, 2 * rows, PAIR), BF),
        vmem((HEADS, PAIR, 2 * rows), BF),
        vmem((2 * rows, PAIR), BF),
        vmem((2 * rows, 512), BF),
        vmem((2 * rows, 512), BF),
        vmem((2 * rows, 576), BF),
        vmem((HEADS, rows, PAIR), F32),
        vmem((WIDE, 2 * rows), BF),
        vmem((WIDE, D), F32),
    )

    def finish(x, qkv_m, proj_m, up_m, down_m, *scratch):
        for_tail = copies(tail_sources, (x, qkv_m, proj_m, up_m, down_m), 12)
        for copy in for_tail:
            copy.start()
        leave = pltpu.make_async_copy(gsec, ingrad_out, copy_sems.at[1])
        tail_phase(
            clips, one, two, arrival(for_tail), leave.start, gnorm, own, across_rows, bsum, tok,
            gsec, x, side_ref, cells_ref, taps_ref, vec_ref, mid_sums, one_ref, two_ref, qkv_m,
            proj_m, up_m, down_m, late_ref, scaled_ref, vsum_ref, *tail_landing, *scratch, early,
            *tail_sems,
        )
        leave.wait()

    pl.run_scoped(
        finish,
        *(vmem(ref.shape, ref.dtype) for ref in tail_sources),
        vmem((owned, D), F32),
        vmem((3, 4, 400, D), F32),
        vmem((3, 4, 440, D), F32),
    )
    out_copy.wait()


def rest(mid_inputs, small, back_inputs, tail_inputs, clips, collective_id):
    rows, block = 800, 3 * D // 4
    chunk = share_rows(block, clips)
    owners = -(-block // chunk)
    vector_shape = (40, D)
    vmem = pltpu.VMEM
    dma = pltpu.SemaphoreType.DMA
    parts = [part.stop - part.start for part in EARLY_PARTS]
    hbm = pl.BlockSpec(memory_space=pl.ANY)
    return pl.pallas_call(
        functools.partial(rest_kernel, clips),
        in_specs=[hbm] * 4
        + [pl.BlockSpec(memory_space=pltpu.SMEM)]
        + [VMEM_SPEC] * 4
        + [hbm] * (len(back_inputs) + len(tail_inputs)),
        out_specs=[hbm] * 2 + [VMEM_SPEC] * 5,
        out_shape=[
            jax.ShapeDtypeStruct(mid_inputs[2].shape, BF),
            jax.ShapeDtypeStruct((rows, D), F32),
        ]
        + [
            jax.ShapeDtypeStruct((clips * share_rows(part, clips), D), BF) for part in parts
        ]
        + [
            jax.ShapeDtypeStruct((owners * chunk, D), F32),
            jax.ShapeDtypeStruct((4, SHARE, D), BF),
            jax.ShapeDtypeStruct(vector_shape, F32),
        ],
        scratch_shapes=[
            vmem((rows, D), F32),
            vmem(mid_inputs[2].shape, BF),
            vmem((rows, D), F32),
            vmem((HEADS, rows, PAIR), BF),
            vmem((4, (D + 2 * FF) // 4, D), BF),
            vmem((8, D), F32),
        ]
        + [vmem(ref.shape, ref.dtype) for ref in back_inputs]
        + [
            vmem((rows, D), F32),
            vmem((block, D), F32),
            vmem((block, D), BF),
            vmem((2, HEADS, 1, PAIR), F32),
            vmem((4, block, D), BF),
            vmem((2, block, D), BF),
            vmem((rows, D), BF),
            vmem((2, rows, D), BF),
            vmem((rows, D), BF),
            vmem((rows, D), BF),
            dma((2, 2)),
            dma((2,)),
            dma((2, 2)),
            vmem((block, D), BF),
            vmem((owners, chunk, D), BF),
            vmem((clips, chunk, D), BF),
            vmem((owners, chunk, D), F32),
            vmem((chunk, D), BF),
            vmem((2, 400, D), BF),
            vmem((2, 400, D), BF),
            vmem(vector_shape, F32),
            vmem((4,) + vector_shape, F32),
            vmem(vector_shape, F32),
            vmem((clips,) + vector_shape, F32),
            vmem((4, SHARE, D), BF),
            dma((2,)),
            dma((2, clips)),
            dma((2, clips)),
            dma((5, clips)),
            dma((2, 2)),
            dma((2, 3)),
            dma((2, clips)),
            dma((2, 4)),
            dma((2, 4)),
            dma((17,)),
        ]
        + row_sums_scratch(parts[0], clips)
        + row_sums_scratch(parts[1], clips),
        compiler_params=pltpu.CompilerParams(
            collective_id=collective_id, has_side_effects=True, vmem_limit_bytes=63 * 2**20
        ),
        cost_estimate=pl.CostEstimate(
            flops=2**36, bytes_accessed=32 * 2**20, transcendentals=2**25
        ),
    )(*mid_inputs, *small, *back_inputs, *tail_inputs)


def adamw(param, mean_old, square_old, gradient, rate_value, decay):
    mean_new = 0.9 * mean_old + 0.1 * gradient
    square_new = 0.999 * square_old + 0.001 * gradient * gradient
    mean_hat = mean_new / (1.0 - 0.9**STEP)
    square_hat = square_new / (1.0 - 0.999**STEP)
    return (
        mean_new,
        square_new,
        param - rate_value * (mean_hat / (jnp.sqrt(square_hat) + 1e-08) + decay * param),
    )


RATES = (0.2 * math.sqrt(3.0), 0.12 * math.sqrt(CLIP_TOK), 0.2 * math.sqrt(FF / D), 0.2)


def update_kernel(*refs):
    refs = list(refs)

    def take(count):
        taken, refs[:count] = refs[:count], []
        return taken

    large_in, (vsum_ref,), vectors, taps, biases = take(13), take(1), take(3), take(3), take(3)
    large_out, new_vectors, new_taps, new_biases = take(10), take(3), take(3), take(3)
    large, made, in_sems, out_sems = take(13), take(9), *take(2)
    arriving = [
        pltpu.make_async_copy(src, dst, in_sems.at[k])
        for k, (src, dst) in enumerate(zip(large_in, large))
    ]
    block, late_ref, one_ref, two_ref = large[:4]
    moments, scaled_ref, weights, ingrad_ref = large[4:7], large[7], large[8:12], large[12]
    leaving = [
        pltpu.make_async_copy(src, dst, out_sems.at[k])
        for k, (src, dst) in enumerate(zip([block] + made, large_out))
    ]
    new_moments, new_weights, out_ref = made[0:4], made[4:8], made[8]
    for copy in arriving:
        copy.start()

    def arrive(*numbers):
        for number in numbers:
            arriving[number].wait()

    arrive(0)
    leaving[0].start()
    arrive(1)
    new_moments[0][...] = late_ref[0 : weights[0].shape[1], :].T
    leaving[1].start()
    arrive(2, 3)
    for which in (1, 2, 3):
        arrive(3 + which)
        rows = weights[which].shape[0]
        summed = one_ref[80:400, :] if which == 2 else (two_ref if which == 3 else one_ref)[0:rows, :]
        new_moments[which][...] = 0.95 * moments[which - 1][...] + summed.astype(F32)
        leaving[1 + which].start()
    arrive(7)
    for which in range(4):
        arrive(8 + which)
        rows = weights[which].shape[1 if which == 0 else 0]
        scaled = scaled_ref[which, 0:rows, :].astype(F32)
        if which == 0:
            scaled = scaled.T
        new_weights[which][...] = 0.999 * weights[which][...] - RATES[which] * scaled
        leaving[5 + which].start()
    arrive(12)
    for row in range(20):
        at = slice(20 * row, 20 * row + 20), slice(400 + 20 * row, 420 + 20 * row)
        out_ref[0, row] = jnp.stack([ingrad_ref[part, :] for part in at], axis=1)
    leaving[9].start()
    bias_sums = vsum_ref[9:13, :]

    def bias_part(part):
        row, column = divmod(part * HEAD_DIM, D)
        return bias_sums[row : row + 1, column : column + HEAD_DIM]

    bias_grad = jnp.concatenate(
        [
            jnp.concatenate([bias_part(2 * r), bias_part(2 * r + 1)], axis=1)
            for r in range(FF // 128)
        ],
        axis=0,
    )
    for (param, mean, square), outs, grad, rate, decay in (
        (vectors, new_vectors, vsum_ref[0:9, :], 0.2, 0.0),
        (taps, new_taps, vsum_ref[13:40, :], 0.05, 0.01),
        (biases, new_biases, bias_grad, 0.2, 0.0),
    ):
        for ref, value in zip(
            outs, adamw(param[...], mean[...], square[...], grad, rate, decay)
        ):
            ref[...] = value
    for copy in leaving:
        copy.wait()


def update(block, sums, weights, moments, vectors, taps, biases):
    ingrad, late, one, two, scaled, vector_sums = sums
    large = [block, late, one, two, *moments[1:], scaled, *weights, ingrad]
    small = [vector_sums, *vectors, *taps, *biases]
    hbm = pl.BlockSpec(memory_space=pl.ANY)
    made = [jax.ShapeDtypeStruct(x.shape, F32) for x in (*moments, *weights, block)]
    outs = [jax.ShapeDtypeStruct(block.shape, BF), *made]
    outs += [jax.ShapeDtypeStruct(x.shape, F32) for x in small[1:]]
    return pl.pallas_call(
        update_kernel,
        in_specs=[hbm] * len(large) + [VMEM_SPEC] * len(small),
        out_specs=[hbm] * 10 + [VMEM_SPEC] * 9,
        out_shape=outs,
        scratch_shapes=[pltpu.VMEM(x.shape, x.dtype) for x in large]
        + [pltpu.VMEM(x.shape, x.dtype) for x in made]
        + [pltpu.SemaphoreType.DMA((len(large),)), pltpu.SemaphoreType.DMA((10,))],
        compiler_params=pltpu.CompilerParams(vmem_limit_bytes=62 * 2**20),
        cost_estimate=pl.CostEstimate(
            flops=2**22, bytes_accessed=12 * 2**20, transcendentals=2**14
        ),
    )(*large, *small)


def frames_last(block):
    return jnp.transpose(block, (0, 2, 3, 1, 4))


def frames_second(block):
    return jnp.transpose(block, (0, 3, 1, 2, 4))


def per_device(
    clips_in,
    out_grad,
    clip_side,
    qkv_weight,
    proj_weight,
    up_weight,
    down_weight,
    qkv_moment,
    proj_moment,
    up_moment,
    down_moment,
    vectors,
    vector_mean,
    vector_square,
    up_bias,
    up_bias_mean,
    up_bias_square,
    conv_kernel,
    kernel_mean,
    kernel_square,
):
    clips = lax.axis_size("clip")
    clips_in, out_grad = frames_last(clips_in), frames_last(out_grad)
    weights = (qkv_weight, proj_weight, up_weight, down_weight)
    moments = (qkv_moment, proj_moment, up_moment, down_moment)
    (
        tokens,
        normed_home,
        normed_cross,
        heads_q,
        home,
        cross,
        kept,
        heads_out,
        query_weight,
        pair_weight,
        other_weights,
    ) = front(clips_in, clip_side, qkv_weight.T, *weights[1:], vectors, conv_kernel, clips, 0)
    block_out, ingrad, sums_one, sums_two, late_moment, scaled, vector_sums = rest(
        (heads_out, tokens, out_grad, other_weights),
        (clip_side, jnp.asarray(CELL_AT), vectors, up_bias.reshape(FF // 128, 128), conv_kernel),
        (
            heads_q,
            kept,
            cross,
            home,
            normed_home,
            normed_cross,
            query_weight,
            pair_weight,
        ),
        (clips_in, qkv_moment.T, *moments[1:]),
        clips,
        1,
    )
    as_rows = lambda vector: vector.reshape(FF // 128, 128)
    updated = update(
        block_out,
        (ingrad, late_moment, sums_one, sums_two, scaled, vector_sums),
        (qkv_weight.T, *weights[1:]),
        (qkv_moment.T, *moments[1:]),
        (vectors, vector_mean, vector_square),
        (conv_kernel, kernel_mean, kernel_square),
        tuple(as_rows(vector) for vector in (up_bias, up_bias_mean, up_bias_square)),
    )
    new_moments = (updated[1].T, *updated[2:5])
    new_weights = (updated[5].T, *updated[6:9])
    outs = [frames_second(updated[0]), frames_second(updated[9])]
    for moment, weight in zip(new_moments, new_weights):
        outs += [moment, weight]
    bias_new = [vector.reshape(FF) for vector in updated[16:19]]
    return (*outs, *updated[10:13], *bias_new, *updated[13:16])


def solution(mesh):
    big = P("clip", "frame", None, None, None)
    rows = P("frame", None)
    return jax.shard_map(
        per_device,
        mesh=mesh,
        in_specs=(big, big, P("clip")) + (rows,) * 8 + (P(),) * 9,
        out_specs=(big, big) + (rows,) * 8 + (P(),) * 9,
        check_vma=False,
    )
```

profile of v0, /device:TPU:1, one launch (start us, length us, event | category | flops | bytes accessed | tf_op | source)
XLA Modules:
  0.0 175.9 jit_solution(10546899836139621854)
XLA Ops:
  1.3 64.9 %shard_map.348 = (f32[800,320]{1,0:T(8,128)}, bf16[1600,320]{1,0:T(8,128)(2,1)}, bf16[1600,320]{1,0:T(8,128)(2,1)}, bf16[5,800,128]{2,1,0:T(8,128)(2,1)}, bf16[5...) custom-call(bf16[1,20,20,2,320]{4,3,2,1,0:T(2,128)(2,1)} %bitcast.21, ...), custom_call_target="tpu_custom_call" | custom-call | flops 17179869184 | bytes 16777216 | tf_op jit(solution)/shard_map/pallas_call | solution.py:548
  66.2 101.8 %shard_map.349 = (bf16[1,20,20,2,320]{4,3,2,1,0:T(2,128)(2,1)}, f32[800,320]{1,0:T(8,128)}, bf16[512,320]{1,0:T(8,128)(2,1)}, bf16[384,320]{1,0:T(8,128)(2,1)}, ...) custom-call(bf16[5,800,128]{2,1,0:T(8,128)(2,1)} %get-tuple-element.56.att_in, ...), custom_call_target="tpu_custom_call" | custom-call | flops 68719476736 | bytes 33554432 | tf_op jit(solution)/shard_map/pallas_call | solution.py:1602
  168.0 7.7 %shard_map.350 = (bf16[1,20,20,2,320]{4,3,2,1,0:T(2,128)(2,1)}, f32[320,240]{1,0:T(8,128)}, f32[80,320]{1,0:T(8,128)}, f32[320,320]{1,0:T(8,128)}, f32[320,320]{...) custom-call(bf16[1,20,20,2,320]{4,3,2,1,0:T(2,128)(2,1)} %get-tuple-, ...), custom_call_target="tpu_custom_call" | custom-call | flops 4194304 | bytes 12582912 | tf_op jit(solution)/shard_map/pallas_call | solution.py:1781
where the time goes:
time: 179 us; the launch traced here: 176 us
  Pallas kernels  174 us (97%)
    pallas_call x1, Pallas kernels, rest(): pl.pallas_call(functools.partial(rest_kernel, clips), in_specs=[hbm] * 4...  102 us
    pallas_call x1, Pallas kernels, front(): pl.pallas_call(functools.partial(front_kernel, clips), in_specs=[VMEM_SPE...  64.9 us
    pallas_call x1, Pallas kernels, update(): pl.pallas_call(update_kernel, in_specs=[hbm] * len(large) + [VMEM_SPEC] *...  7.71 us

commit v1 on v0

--- a/solution.py
+++ b/solution.py
@@ -376,7 +376,7 @@
         near_sems.at[1],
         near,
     )
-    for t, depths, ready in ((0, (0,), (0, 1)), (1, (2,), (2, 3, 4))):
+    for t, depths, ready in ((0, (0,), (0, 1)), (1, (2,), (2,))):
 
         def rim_part(step, carry, t=t, depths=depths):
             start = pl.multiple_of(step * 40, 8)
@@ -441,6 +441,7 @@
         cross_ref[h] = value
 
     project(nhome_ref[0:rows, :], wq_ref, wide_query, place_query)
+    cross_copy(3).start()
     project(nhome_ref[0:rows, :], wkv_ref, wide_pair, place_own)
     leave(q_ref, q_out)
     tail[...] = tail_lanes(inside, 4)
@@ -501,6 +502,7 @@
     near_copy.wait_recv()
     other_near.wait()
     leave(nhome_ref, nhome_out)
+    cross_copy(4).start()
     project(nhome_ref[rows : 2 * rows, :], wkv_ref, wide_pair, place_near)
     leave(home_ref, home_out)
     lax.fori_loop(0, 2, first_pass, 0)
@@ -930,6 +932,9 @@
         @pl.when(h == 0)
         def _():
             one.cross_step()
+
+        @pl.when(h == 2)
+        def _():
             two.cross_step()
 
         @pl.when(h == 3)
@@ -1149,27 +1154,6 @@
     other_owners(lambda owner: part_copy(owner).start())
     start_halos(down, up, rim)
 
-    moments = (None, proj_m_ref, up_m_ref, down_m_ref)
-
-    def to_owner(which):
-        at = pl.ds(0, moments[which].shape[0])
-        return send(
-            low.at[which, at, :],
-            gathered.at[f, at, :],
-            there_sems.at[0, which],
-            there_sems.at[1, f],
-            OWNER_OF[which],
-        )
-
-    for which in (3, 2, 1):
-        rows = moments[which].shape[0]
-        summed = one_ref[80:400, :] if which == 2 else (two_ref if which == 3 else one_ref)[0:rows, :]
-        low[which, 0:rows, :] = (0.95 * moments[which][...] + summed.astype(F32)).astype(BF)
-
-        @pl.when(f != OWNER_OF[which])
-        def _(which=which):
-            to_owner(which).start()
-
     def row_copy(clip):
         return pltpu.make_async_remote_copy(
             src_ref=new_rows.at[c],
@@ -1261,6 +1245,28 @@
                 v_mine[at, :] = column_sum(total)
 
     plane(0, 0, False, False)
+
+    moments = (None, proj_m_ref, up_m_ref, down_m_ref)
+
+    def to_owner(which):
+        at = pl.ds(0, moments[which].shape[0])
+        return send(
+            low.at[which, at, :],
+            gathered.at[f, at, :],
+            there_sems.at[0, which],
+            there_sems.at[1, f],
+            OWNER_OF[which],
+        )
+
+    for which in (3, 2, 1):
+        rows = moments[which].shape[0]
+        summed = one_ref[80:400, :] if which == 2 else (two_ref if which == 3 else one_ref)[0:rows, :]
+        low[which, 0:rows, :] = (0.95 * moments[which][...] + summed.astype(F32)).astype(BF)
+
+        @pl.when(f != OWNER_OF[which])
+        def _(which=which):
+            to_owner(which).start()
+
     plane(0, 1, True, False)
     share_sum()
     plane(1, 1, False, True)
@@ -1697,53 +1703,32 @@
         taken, refs[:count] = refs[:count], []
         return taken
 
-    large_in, (vsum_ref,), vectors, taps, biases = take(13), take(1), take(3), take(3), take(3)
-    large_out, new_vectors, new_taps, new_biases = take(10), take(3), take(3), take(3)
-    large, made, in_sems, out_sems = take(13), take(9), *take(2)
-    arriving = [
-        pltpu.make_async_copy(src, dst, in_sems.at[k])
-        for k, (src, dst) in enumerate(zip(large_in, large))
-    ]
-    block, late_ref, one_ref, two_ref = large[:4]
-    moments, scaled_ref, weights, ingrad_ref = large[4:7], large[7], large[8:12], large[12]
-    leaving = [
-        pltpu.make_async_copy(src, dst, out_sems.at[k])
-        for k, (src, dst) in enumerate(zip([block] + made, large_out))
-    ]
-    new_moments, new_weights, out_ref = made[0:4], made[4:8], made[8]
-    for copy in arriving:
-        copy.start()
-
-    def arrive(*numbers):
-        for number in numbers:
-            arriving[number].wait()
-
-    arrive(0)
-    leaving[0].start()
-    arrive(1)
-    new_moments[0][...] = late_ref[0 : weights[0].shape[1], :].T
-    leaving[1].start()
-    arrive(2, 3)
+    block_in, ingrad_ref, late_ref, one_ref, two_ref, scaled_ref, vsum_ref = take(7)
+    weights, moments, vectors, taps, biases = take(4), take(3), take(3), take(3), take(3)
+    block_out, out_ref = take(2)
+    new_moments, new_weights = take(4), take(4)
+    new_vectors, new_taps, new_biases = take(3), take(3), take(3)
+    block, sem = take(2)
+    into = pltpu.make_async_copy(block_in, block, sem)
+    into.start()
+    for row in range(20):
+        at = slice(20 * row, 20 * row + 20), slice(400 + 20 * row, 420 + 20 * row)
+        out_ref[0, row] = jnp.stack([ingrad_ref[part, :] for part in at], axis=1)
+    into.wait()
+    through = pltpu.make_async_copy(block, block_out, sem)
+    through.start()
+    rows = weights[0].shape[1]
+    new_moments[0][...] = late_ref[0:rows, :].T
+    new_weights[0][...] = 0.999 * weights[0][...] - RATES[0] * (
+        scaled_ref[0, 0:rows, :].astype(F32).T
+    )
     for which in (1, 2, 3):
-        arrive(3 + which)
         rows = weights[which].shape[0]
         summed = one_ref[80:400, :] if which == 2 else (two_ref if which == 3 else one_ref)[0:rows, :]
         new_moments[which][...] = 0.95 * moments[which - 1][...] + summed.astype(F32)
-        leaving[1 + which].start()
-    arrive(7)
-    for which in range(4):
-        arrive(8 + which)
-        rows = weights[which].shape[1 if which == 0 else 0]
-        scaled = scaled_ref[which, 0:rows, :].astype(F32)
-        if which == 0:
-            scaled = scaled.T
-        new_weights[which][...] = 0.999 * weights[which][...] - RATES[which] * scaled
-        leaving[5 + which].start()
-    arrive(12)
-    for row in range(20):
-        at = slice(20 * row, 20 * row + 20), slice(400 + 20 * row, 420 + 20 * row)
-        out_ref[0, row] = jnp.stack([ingrad_ref[part, :] for part in at], axis=1)
-    leaving[9].start()
+        new_weights[which][...] = 0.999 * weights[which][...] - RATES[which] * scaled_ref[
+            which, 0:rows, :
+        ].astype(F32)
     bias_sums = vsum_ref[9:13, :]
 
     def bias_part(part):
@@ -1766,31 +1751,28 @@
             outs, adamw(param[...], mean[...], square[...], grad, rate, decay)
         ):
             ref[...] = value
-    for copy in leaving:
-        copy.wait()
+    through.wait()
 
 
 def update(block, sums, weights, moments, vectors, taps, biases):
-    ingrad, late, one, two, scaled, vector_sums = sums
-    large = [block, late, one, two, *moments[1:], scaled, *weights, ingrad]
-    small = [vector_sums, *vectors, *taps, *biases]
+    operands = [block, *sums, *weights, *moments[1:], *vectors, *taps, *biases]
     hbm = pl.BlockSpec(memory_space=pl.ANY)
-    made = [jax.ShapeDtypeStruct(x.shape, F32) for x in (*moments, *weights, block)]
-    outs = [jax.ShapeDtypeStruct(block.shape, BF), *made]
-    outs += [jax.ShapeDtypeStruct(x.shape, F32) for x in small[1:]]
+    outs = [jax.ShapeDtypeStruct(block.shape, dtype) for dtype in (BF, F32)]
+    outs += [
+        jax.ShapeDtypeStruct(x.shape, F32)
+        for x in (*moments, *weights, *vectors, *taps, *biases)
+    ]
     return pl.pallas_call(
         update_kernel,
-        in_specs=[hbm] * len(large) + [VMEM_SPEC] * len(small),
-        out_specs=[hbm] * 10 + [VMEM_SPEC] * 9,
+        in_specs=[hbm] + [VMEM_SPEC] * (len(operands) - 1),
+        out_specs=[hbm] + [VMEM_SPEC] * (len(outs) - 1),
         out_shape=outs,
-        scratch_shapes=[pltpu.VMEM(x.shape, x.dtype) for x in large]
-        + [pltpu.VMEM(x.shape, x.dtype) for x in made]
-        + [pltpu.SemaphoreType.DMA((len(large),)), pltpu.SemaphoreType.DMA((10,))],
+        scratch_shapes=[pltpu.VMEM(block.shape, BF), pltpu.SemaphoreType.DMA],
         compiler_params=pltpu.CompilerParams(vmem_limit_bytes=62 * 2**20),
         cost_estimate=pl.CostEstimate(
             flops=2**22, bytes_accessed=12 * 2**20, transcendentals=2**14
         ),
-    )(*large, *small)
+    )(*operands)
 
 
 def frames_last(block):
@@ -1867,9 +1849,9 @@
         (conv_kernel, kernel_mean, kernel_square),
         tuple(as_rows(vector) for vector in (up_bias, up_bias_mean, up_bias_square)),
     )
-    new_moments = (updated[1].T, *updated[2:5])
-    new_weights = (updated[5].T, *updated[6:9])
-    outs = [frames_second(updated[0]), frames_second(updated[9])]
+    new_moments = (updated[2].T, *updated[3:6])
+    new_weights = (updated[6].T, *updated[7:10])
+    outs = [frames_second(updated[0]), frames_second(updated[1])]
     for moment, weight in zip(new_moments, new_weights):
         outs += [moment, weight]
     bias_new = [vector.reshape(FF) for vector in updated[16:19]]

time: 179 us -> 177 us (0.989)
  no operation moved by 1% of the time
where the time goes in v1:
time: 177 us; the launch traced here: 175 us
  Pallas kernels  173 us (98%)
    pallas_call x1, Pallas kernels, rest(): pl.pallas_call(functools.partial(rest_kernel, clips), in_specs=[hbm] * 4...  101 us
    pallas_call x1, Pallas kernels, front(): pl.pallas_call(functools.partial(front_kernel, clips), in_specs=[VMEM_SPE...  65 us
    pallas_call x1, Pallas kernels, update(): pl.pallas_call(update_kernel, in_specs=[hbm] + [VMEM_SPEC] * (len(operand...  6.77 us

profile of v1, /device:TPU:1, one launch (start us, length us, event | category | flops | bytes accessed | tf_op | source)
XLA Modules:
  0.0 174.6 jit_solution(14204686146270463069)
XLA Ops:
  1.3 65.0 %shard_map.348 = (f32[800,320]{1,0:T(8,128)}, bf16[1600,320]{1,0:T(8,128)(2,1)}, bf16[1600,320]{1,0:T(8,128)(2,1)}, bf16[5,800,128]{2,1,0:T(8,128)(2,1)}, bf16[5...) custom-call(bf16[1,20,20,2,320]{4,3,2,1,0:T(2,128)(2,1)} %bitcast.21, ...), custom_call_target="tpu_custom_call" | custom-call | flops 17179869184 | bytes 16777216 | tf_op jit(solution)/shard_map/pallas_call | solution.py:550
  66.3 101.3 %shard_map.349 = (bf16[1,20,20,2,320]{4,3,2,1,0:T(2,128)(2,1)}, f32[800,320]{1,0:T(8,128)}, bf16[512,320]{1,0:T(8,128)(2,1)}, bf16[384,320]{1,0:T(8,128)(2,1)}, ...) custom-call(bf16[5,800,128]{2,1,0:T(8,128)(2,1)} %get-tuple-element.56.att_in, ...), custom_call_target="tpu_custom_call" | custom-call | flops 68719476736 | bytes 33554432 | tf_op jit(solution)/shard_map/pallas_call | solution.py:1608
  167.6 6.8 %shard_map.350 = (bf16[1,20,20,2,320]{4,3,2,1,0:T(2,128)(2,1)}, f32[1,20,20,2,320]{4,3,2,1,0:T(2,128)}, f32[320,240]{1,0:T(8,128)}, f32[80,320]{1,0:T(8,128)}, f...) custom-call(bf16[1,20,20,2,320]{4,3,2,1,0:T(2,128)(2,1)} %get-tuple-, ...), custom_call_target="tpu_custom_call" | custom-call | flops 4194304 | bytes 12582912 | tf_op jit(solution)/shard_map/pallas_call | solution.py:1765
